TPU v7x, 32 devices: a whole 2x2x4 slice. The times are simulated.
32 devices in a mesh: centre: 8 (over z, y), row: 4 (over x, core).
Axes of the slice: x: 2, y: 2, z: 4, core: 2. Of those that a mesh axis runs over, the one named last changes fastest.
Arguments:
- pool: bfloat16 [1024, 16384], P('centre', 'row')
- batch_index: int32 [1024], P('row'), may hold values from 0 to 16383, as said below
- targets: float32 [10, 1024], P(None, 'row'), may hold values from -6 to 6
- centres: bfloat16 [65536, 1024], P(('centre', 'row'))
- weights: float32 [10, 65536], P(None, ('centre', 'row')), may hold values from -0.0234375 to 0.0234375
- sample_index: int32 [512], P(('centre', 'row')), may hold values from 0 to 65535, as said below
- factor: float32 [512, 128], P(('centre', 'row')), may hold values from -0.5 to 0.5
Outputs:
- gradient: float32 [10, 1024], P(None, 'row')
- update: float32 [10, 512], P(None, ('centre', 'row'))
Inputs may be any that keep to these rules, and one draw needn't show every extreme that they name: `batch_index`: the entries at positions r * 256 to (r + 1) * 256 - 1 lie in r * 4096 to (r + 1) * 4096 - 1; repeats may occur. `sample_index`: all entries differ; the entries at positions k * 16 to (k + 1) * 16 - 1 lie in k * 2048 to (k + 1) * 2048 - 1.
All inputs are finite; a program needn't handle non-finite values.
Results may differ from a plain program's by a relative error of at most 0.0003.
Values may be sent and summed in bfloat16 or wider, within the bound.
A program may use at most 128 MiB of HBM per device.

v0:
```python
import math
import jax
import jax.numpy as jnp
from jax import lax
from jax.sharding import PartitionSpec as P

PROJ_STEPS = 2
EPS = 1e-06
HIGH = lax.Precision.HIGHEST


def row_scale(rows, axis):
    values = rows.astype(jnp.float32)
    return jnp.sqrt(jnp.mean(values * values, axis=axis) + EPS)


def tangent_kernel(inner, left_scale, right_scale, width):
    product = left_scale[:, None] * right_scale[None, :]
    cosine = jnp.clip(inner / (width * product), -1.0, 1.0)
    angle = jnp.arccos(cosine)
    first = (math.pi - angle) / math.pi
    second = (cosine * (math.pi - angle) + jnp.sqrt(1.0 - cosine * cosine)) / math.pi
    return product * (second + cosine * first)


def on_device(pool, batch_index, targets, centres, weights, sample_index, factor):
    width = float(centres.shape[1])
    labels = weights.shape[0]
    rows_dev = batch_index.shape[0]
    pool_dev = pool.shape[1]
    cent_dev = centres.shape[0]
    samp_dev = sample_index.shape[0]
    row_count = lax.axis_size("row")
    total_rows = rows_dev * row_count
    total_samp = samp_dev * row_count * lax.axis_size("centre")
    contract = (((1,), (1,)), ((), ()))
    local_batch = batch_index - lax.axis_index("row") * pool_dev
    picked = jnp.take(pool, local_batch, axis=1)
    features = lax.all_gather(picked, "centre", axis=0, tiled=True)
    all_targets = lax.all_gather(targets, "row", axis=1, tiled=True)
    centre_scale = row_scale(centres, 1)
    local_sample = sample_index - lax.axis_index(("centre", "row")) * cent_dev
    sample_rows = jnp.take(centres, local_sample, axis=0)
    sample_scale = jnp.take(centre_scale, local_sample)
    piece = lax.all_gather(features, "row", axis=1, tiled=True)
    inner = jnp.dot(centres, piece, preferred_element_type=jnp.float32)
    kernel = tangent_kernel(inner, centre_scale, row_scale(piece, 0), width)
    partial_value = jnp.dot(weights, kernel, precision=HIGH)
    tiles = jnp.concatenate([partial_value, jnp.take(kernel, local_sample, axis=0)], axis=0)
    partial_value = tiles[:labels]
    cross = tiles[labels:]
    totals = lax.psum(partial_value, ("centre", "row"))
    gradient_all = totals - all_targets
    gradient = lax.dynamic_slice_in_dim(gradient_all, lax.axis_index("row") * rows_dev, rows_dev, 1)
    push = lax.dot_general(gradient_all, cross, contract, precision=HIGH) / total_rows
    piece = lax.all_gather(sample_rows, ("centre", "row"), axis=0, tiled=True)
    inner = lax.dot_general(sample_rows, piece, contract, preferred_element_type=jnp.float32)
    block = tangent_kernel(inner, sample_scale, row_scale(piece, 1), width)
    update = jnp.zeros((labels, samp_dev), jnp.float32)
    for step in range(PROJ_STEPS):
        if step == 0:
            slope = push
        else:
            update_whole = lax.all_gather(update, ("centre", "row"), axis=1, tiled=True)
            slope = (
                lax.dot_general(update_whole, block, contract, precision=HIGH) / total_samp + push
            )
        coef = lax.psum(jnp.dot(slope, factor, precision=HIGH), ("centre", "row"))
        update = update - (slope - jnp.dot(coef, factor.T, precision=HIGH))
    return (gradient, update)


def solution(mesh):
    placed = (
        P("centre", "row"),
        P("row"),
        P(None, "row"),
        P(("centre", "row"), None),
        P(None, ("centre", "row")),
        P(("centre", "row")),
        P(("centre", "row"), None),
    )
    return jax.shard_map(
        on_device,
        mesh=mesh,
        in_specs=placed,
        out_specs=(P(None, "row"), P(None, ("centre", "row"))),
        check_vma=False,
    )
```

profile of v0, /device:TPU:10, one launch (start us, length us, event | category | flops | bytes accessed | tf_op | source)
XLA Modules:
  0.0 314.5 jit_solution(3120540883913514165)
XLA Ops:
  7.2 0.0 copy-start
  7.2 0.0 copy-start.3
  7.2 0.0 all-gather.5.cloned.1.call-start
  7.2 0.7 compare_and_fusion
  7.9 3.3 %gather_fusion.3 = bf16[16,1024]{1,0:T(8,128)(2,1)S(1)} fusion(bf16[2048,1024]{1,0:T(8,128)(2,1)} %param.10, s32[1024]{0:T(1024)S(1)} %pad_clamp_fusion), kind=kCustom, calls=%fused_computation.3 | custom fusion | bytes 65600 | tf_op jit(solution)/shard_map/jit(_take)/gather | solution.py:43
  11.3 0.7 broadcast_select_fusion
  11.9 0.0 copy-start.1
  11.9 0.0 all-gather.5.cloned.1.call-update
  12.0 0.0 all-gather.3.cloned.1.call-start
  12.0 1.6 copy.13
  13.6 0.7 compare_and_fusion.1
  14.3 0.9 gather_fusion
  15.2 0.1 select_bitcast_fusion
  15.3 28.9 %all_gather.15 = bf16[1024,256]{0,1:T(8,128)(2,1)} all-gather(bf16[128,256]{0,1:T(8,128)(2,1)S(1)} %select_bitcast_fusion), channel_id=1, replica_groups=mesh['centre'=8,'row'=4] {'centre'}, dimensions={0}, use_global_device_ids=true | all-gather | bytes 589824 | tf_op jit(solution)/shard_map/all_gather | solution.py:39
  44.2 0.0 all-gather.3.cloned.1.call-update
  44.2 3.1 multiply_reduce_fusion
  47.3 0.7 gather_fusion.2
  48.0 0.0 copy-done.3
  48.0 5.2 %all_gather.17 = f32[10,1024]{1,0:T(8,128)S(1)} all-gather(f32[10,256]{1,0:T(8,128)S(1)} %copy-done.3), channel_id=1, replica_groups=mesh['centre'=8,'row'=4] {'row'}, dimensions={1}, use_global_device_ids=true | all-gather | bytes 51200 | tf_op jit(solution)/shard_map/all_gather | solution.py:40
  53.2 13.0 %all-gather.5.cloned.1.call-done = bf16[512,1024]{1,0:T(8,128)(2,1)} async-done(((bf16[16,1024]{1,0:T(8,128)(2,1)}), bf16[512,1024]{1,0:T(8,128)(2,1)}) %all-gather.5.cloned.1.call-update) | async-done | bytes 1048592 | tf_op jit(solution)/shard_map/all_gather | solution.py:56
  66.3 1.5 multiply_reduce_fusion.2
  67.8 0.0 copy-done.1
  67.8 1.6 fusion.2
  69.4 19.9 %all-gather.3.cloned.1.call-done = bf16[1024,1024]{0,1:T(8,128)(2,1)} async-done(((bf16[1024,256]{0,1:T(8,128)(2,1)}), bf16[1024,1024]{0,1:T(8,128)(2,1)}) %all-gather.3.cloned.1.call-update) | async-done | bytes 2097168 | tf_op jit(solution)/shard_map/all_gather | solution.py:45
  89.2 2.1 multiply_reduce_fusion.1
  91.3 29.4 %multiply_multiply_fusion = f32[2048,1024]{0,1:T(8,128)} fusion(bf16[1024,1024]{0,1:T(8,128)(2,1)} %all-gather.3.cloned.1.call-done, bf16[2048,1024]{1,0:T(8,128)(2,1)} %param.10, f32[1024]{0:T(1024)S(1)} %add_sqrt_fusion.1, f32[2048]{0:T(1024)S(1)} %add_sqrt_fusion), kind=kOutput, calls=%fused_computation.4 | convolution fusion | flops 4330618880 | bytes 14692352 | tf_op jit(solution)/shard_map/dot_general | solution.py:46
  120.7 9.3 %copy.14 = f32[2048,1024]{1,0:T(8,128)} copy(f32[2048,1024]{0,1:T(8,128)} %multiply_multiply_fusion) | data formatting | bytes 16777216 | tf_op jit(solution)/shard_map/mul | solution.py:23
  129.9 0.0 copy-start.2
  129.9 4.0 %gather_fusion.1 = f32[16,1024]{1,0:T(8,128)S(1)} fusion(f32[2048,1024]{1,0:T(8,128)} %copy.14, s32[1024]{0:T(1024)S(1)} %pad_clamp_fusion), kind=kCustom, calls=%fused_computation.1 | custom fusion | bytes 131136 | tf_op jit(solution)/shard_map/jit(_take)/gather | solution.py:49
  134.0 0.0 copy-done
  134.0 9.4 %convolution_bitcast_fusion = f32[10,1024]{1,0:T(8,128)S(1)} fusion(f32[2048,1024]{0,1:T(8,128)} %multiply_multiply_fusion, f32[10,2048]{1,0:T(8,128)S(1)} %copy-done), kind=kOutput, calls=%fused_computation.11 | convolution fusion | flops 251658240 | bytes 8511488 | tf_op jit(solution)/shard_map/dot_general | solution.py:48
  143.4 41.3 %psum.21 = f32[10,1024]{1,0:T(8,128)S(1)} all-reduce(f32[10,1024]{1,0:T(8,128)S(1)} %convolution_bitcast_fusion), channel_id=1, replica_groups=mesh['centre'=8,'row'=4] {'centre','row'}, use_global_device_ids=true, to_apply=%region_2.3 | all-reduce | flops 10240 | bytes 81920 | tf_op jit(solution)/shard_map/psum | solution.py:52
  184.7 0.2 convolution_multiply_fusion.1
  185.0 0.0 copy-done.2
  185.0 0.1 fusion.33
  185.1 40.0 %psum.22 = f32[10,128]{1,0:T(8,128)S(1)} all-reduce(f32[10,128]{1,0:T(8,128)S(1)} %fusion.33), channel_id=1, replica_groups=mesh['centre'=8,'row'=4] {'centre','row'}, use_global_device_ids=true, to_apply=%region_3.4 | all-reduce | flops 1280 | bytes 10240 | tf_op jit(solution)/shard_map/psum | solution.py:68
  225.2 0.1 fusion.5
  225.3 0.1 copy.15
  225.4 31.4 %all_gather.18 = f32[10,512]{0,1:T(8,128)S(1)} all-gather(f32[10,16]{0,1:T(8,128)S(1)} %copy.15), channel_id=1, replica_groups=mesh['centre'=8,'row'=4] {'centre','row'}, dimensions={1}, use_global_device_ids=true | all-gather | bytes 21120 | tf_op jit(solution)/shard_map/all_gather | solution.py:64
  256.8 0.6 fusion.4
  257.4 0.1 fusion.34
  257.5 48.8 %psum.23 = f32[10,128]{1,0:T(8,128)S(1)} all-reduce(f32[10,128]{1,0:T(8,128)S(1)} %fusion.34), channel_id=1, replica_groups=mesh['centre'=8,'row'=4] {'centre','row'}, use_global_device_ids=true, to_apply=%region_5.6 | all-reduce | flops 1280 | bytes 10240 | tf_op jit(solution)/shard_map/psum | solution.py:68
  306.4 0.7 fusion.3
  307.1 0.6 constant_dynamic-slice_fusion
  (7 shorter events, 0.1 us)
Async XLA Ops:
  7.2 126.8 %copy-start = (f32[10,2048]{1,0:T(8,128)S(1)}, f32[10,2048]{1,0:T(8,128)}, u32[]{:S(2)}) copy-start(f32[10,2048]{1,0:T(8,128)} %param.11) | copy-start | bytes 245764
  7.2 40.8 %copy-start.3 = (f32[10,256]{1,0:T(8,128)S(1)}, f32[10,256]{1,0:T(8,128)}, u32[]{:S(2)}) copy-start(f32[10,256]{1,0:T(8,128)} %param.9) | copy-start | bytes 30724
  7.2 59.1 %all-gather.5.cloned.1.call-start = ((), (), s32[]{:S(2)}) async-start(), calls=%async_computation.1 | async-start | bytes 1081344 | tf_op jit(solution)/shard_map/all_gather | solution.py:56
  11.9 55.8 %copy-start.1 = (bf16[16,1024]{1,0:T(8,128)(2,1)S(1)}, bf16[16,1024]{1,0:T(8,128)(2,1)}, u32[]{:S(2)}) copy-start(bf16[16,1024]{1,0:T(8,128)(2,1)} %broadcast_select_fusion) | copy-start | bytes 98308
  12.0 77.3 %all-gather.3.cloned.1.call-start = ((), (), s32[]{:S(2)}) async-start(), calls=%async_computation | async-start | bytes 2621440 | tf_op jit(solution)/shard_map/all_gather | solution.py:45
  129.9 55.0 %copy-start.2 = (f32[16,128]{1,0:T(8,128)S(1)}, f32[16,128]{1,0:T(8,128)}, u32[]{:S(2)}) copy-start(f32[16,128]{1,0:T(8,128)} %param.13) | copy-start | bytes 24580
Sparse Core Ops, SparseCore 0:
  12.1 54.1 all-gather.4
  67.8 21.3 all-gather.2
where the time goes:
time: 315 us
  blocking collectives  196 us (62%)
  matrix products  42.3 us (13%)
  waiting for transfers between devices  32.9 us (10%)
  local copies, waits for them, and re-layouts  20.5 us (7%)
  between operations  14.2 us (5%)
  other arithmetic  8.84 us (3%)
    psum x2, blocking collectives, on_device(): coef = lax.psum(jnp.dot(slope, factor, precision=HIGH), ('centre', 'row'))  88.9 us
    psum x1, blocking collectives, on_device(): totals = lax.psum(partial_value, ('centre', 'row'))  41.3 us
    all_gather x1, blocking collectives, on_device(): update_whole = lax.all_gather(update, ('centre', 'row'), axis=1, tiled=True)  31.4 us
    dot_general x1, matrix products, on_device(): inner = jnp.dot(centres, piece, preferred_element_type=jnp.float32)  29.4 us
    all_gather x1, blocking collectives, on_device(): features = lax.all_gather(picked, 'centre', axis=0, tiled=True)  28.9 us
    all_gather x1, waiting for transfers between devices, on_device(): piece = lax.all_gather(features, 'row', axis=1, tiled=True)  19.9 us
    all_gather x1, waiting for transfers between devices, on_device(): piece = lax.all_gather(sample_rows, ('centre', 'row'), axis=0, tiled=True)  13 us
    dot_general x1, matrix products, on_device(): partial_value = jnp.dot(weights, kernel, precision=HIGH)  9.43 us
  transfers between devices with their start and end apart: 2, of which 2 were waited for; matrix products, arithmetic and copies ran while one was open for 3% of the time, Pallas kernels for 0%

commit v1 on v0

--- a/solution.py
+++ b/solution.py
@@ -37,12 +37,15 @@
     local_batch = batch_index - lax.axis_index("row") * pool_dev
     picked = jnp.take(pool, local_batch, axis=1)
     features = lax.all_gather(picked, "centre", axis=0, tiled=True)
-    all_targets = lax.all_gather(targets, "row", axis=1, tiled=True)
     centre_scale = row_scale(centres, 1)
     local_sample = sample_index - lax.axis_index(("centre", "row")) * cent_dev
     sample_rows = jnp.take(centres, local_sample, axis=0)
     sample_scale = jnp.take(centre_scale, local_sample)
-    piece = lax.all_gather(features, "row", axis=1, tiled=True)
+    all_targets, piece = jnp.split(
+        lax.all_gather(jnp.concatenate([targets, features], axis=0), "row", axis=1, tiled=True),
+        [targets.shape[0]],
+        axis=0,
+    )
     inner = jnp.dot(centres, piece, preferred_element_type=jnp.float32)
     kernel = tangent_kernel(inner, centre_scale, row_scale(piece, 0), width)
     partial_value = jnp.dot(weights, kernel, precision=HIGH)

time: 315 us -> 330 us (1.048)
  waiting for transfers between devices: 32.9 us -> 48.2 us
  blocking collectives: 196 us -> 191 us
  other arithmetic: 8.84 us -> 12.2 us
    all_gather x1, waiting for transfers between devices: 19.9 us -> 32.2 us  [on_device(): lax.all_gather(jnp.concatenate([targets, features], axis=0), 'row', axis=...]
    all_gather x1 -> x0, blocking collectives: 5.25 us -> none  [on_device(): all_targets = lax.all_gather(targets, 'row', axis=1, tiled=True)]
  transfers between devices with their start and end apart: 2 -> 2, of which waited for: 2 -> 2; matrix products, arithmetic and copies ran while one was open for 3% -> 4% of each run, Pallas kernels for 0% -> 0%
where the time goes in v1:
time: 330 us; the launch traced here: 329 us
  blocking collectives  191 us (58%)
  waiting for transfers between devices  48.2 us (15%)
  matrix products  43.4 us (13%)
  local copies, waits for them, and re-layouts  20.6 us (6%)
  between operations  14.2 us (4%)
  other arithmetic  12.2 us (4%)
    psum x2, blocking collectives, on_device(): coef = lax.psum(jnp.dot(slope, factor, precision=HIGH), ('centre', 'row'))  89 us
    psum x1, blocking collectives, on_device(): totals = lax.psum(partial_value, ('centre', 'row'))  41.3 us
    all_gather x1, waiting for transfers between devices, on_device(): lax.all_gather(jnp.concatenate([targets, features], axis=0), 'row', axis=...  32.2 us
    all_gather x1, blocking collectives, on_device(): update_whole = lax.all_gather(update, ('centre', 'row'), axis=1, tiled=True)  31.4 us
    dot_general x1, matrix products, on_device(): inner = jnp.dot(centres, piece, preferred_element_type=jnp.float32)  30.4 us
    all_gather x1, blocking collectives, on_device(): features = lax.all_gather(picked, 'centre', axis=0, tiled=True)  29.2 us
    all_gather x1, waiting for transfers between devices, on_device(): piece = lax.all_gather(sample_rows, ('centre', 'row'), axis=0, tiled=True)  16 us
    dot_general x1, matrix products, on_device(): partial_value = jnp.dot(weights, kernel, precision=HIGH)  9.43 us
  transfers between devices with their start and end apart: 2, of which 2 were waited for; matrix products, arithmetic and copies ran while one was open for 4% of the time, Pallas kernels for 0%

profile of v1, /device:TPU:10, one launch (start us, length us, event | category | flops | bytes accessed | tf_op | source)
XLA Modules:
  0.0 329.5 jit_solution(9459336118811070634)
XLA Ops:
  7.2 0.0 copy-start
  7.2 0.0 all-gather.5.cloned.1.call-start
  7.2 0.7 compare_and_fusion
  7.9 3.3 %gather_fusion.3 = bf16[16,1024]{1,0:T(8,128)(2,1)S(1)} fusion(bf16[2048,1024]{1,0:T(8,128)(2,1)} %param.10, s32[1024]{0:T(1024)S(1)} %pad_clamp_fusion), kind=kCustom, calls=%fused_computation.3 | custom fusion | bytes 65600 | tf_op jit(solution)/shard_map/jit(_take)/gather | solution.py:42
  11.3 0.7 broadcast_select_fusion
  11.9 0.0 copy-start.1
  11.9 0.0 all-gather.5.cloned.1.call-update
  12.0 0.0 all-gather.3.cloned.1.call-start
  12.0 1.6 copy.15
  13.6 0.7 compare_and_fusion.1
  14.3 0.9 gather_fusion
  15.2 0.1 copy.16
  15.3 29.2 %all_gather.12 = bf16[1024,256]{1,0:T(8,128)(2,1)S(1)} all-gather(bf16[128,256]{1,0:T(8,128)(2,1)S(1)} %select_bitcast_fusion), channel_id=1, replica_groups=mesh['centre'=8,'row'=4] {'centre'}, dimensions={0}, use_global_device_ids=true | all-gather | bytes 589824 | tf_op jit(solution)/shard_map/all_gather | solution.py:39
  44.6 0.1 convert_element_type.10
  44.6 1.8 pad_maximum_fusion
  46.4 0.0 all-gather.3.cloned.1.call-update
  46.4 3.1 multiply_reduce_fusion
  49.5 0.7 gather_fusion.2
  50.2 16.0 %all-gather.5.cloned.1.call-done = bf16[512,1024]{1,0:T(8,128)(2,1)} async-done(((bf16[16,1024]{1,0:T(8,128)(2,1)}), bf16[512,1024]{1,0:T(8,128)(2,1)}) %all-gather.5.cloned.1.call-update) | async-done | bytes 1048592 | tf_op jit(solution)/shard_map/all_gather | solution.py:59
  66.2 1.5 multiply_reduce_fusion.2
  67.7 0.0 copy-done.1
  67.7 1.6 fusion.3
  69.3 32.2 %all-gather.3.cloned.1.call-done = f32[1034,1024]{1,0:T(8,128)} async-done(((f32[1034,256]{1,0:T(8,128)}), f32[1034,1024]{1,0:T(8,128)}) %all-gather.3.cloned.1.call-update) | async-done | bytes 4235280 | tf_op jit(solution)/shard_map/all_gather | solution.py:45
  101.5 2.8 multiply_reduce_fusion.1
  104.3 30.4 %multiply_multiply_fusion = f32[2048,1024]{0,1:T(8,128)} fusion(bf16[2048,1024]{1,0:T(8,128)(2,1)} %param.10, f32[1024]{0:T(1024)S(1)} %add_sqrt_fusion.1, f32[2048]{0:T(1024)S(1)} %add_sqrt_fusion, f32[1034,1024]{1,0:T(8,128)} %all-gather.3.cloned.1.call-done), kind=kOutput, calls=%fused_computation.4 | convolution fusion | flops 4330618880 | bytes 14692352 | tf_op jit(solution)/shard_map/dot_general | solution.py:49
  134.7 9.3 %copy.17 = f32[2048,1024]{1,0:T(8,128)} copy(f32[2048,1024]{0,1:T(8,128)} %multiply_multiply_fusion) | data formatting | bytes 16777216 | tf_op jit(solution)/shard_map/mul | solution.py:23
  144.0 0.0 copy-done
  144.0 0.0 copy-start.2
  144.0 9.4 %convolution_bitcast_fusion = f32[10,1024]{1,0:T(8,128)S(1)} fusion(f32[2048,1024]{0,1:T(8,128)} %multiply_multiply_fusion, f32[10,2048]{1,0:T(8,128)S(1)} %copy-done), kind=kOutput, calls=%fused_computation.12 | convolution fusion | flops 251658240 | bytes 8511488 | tf_op jit(solution)/shard_map/dot_general | solution.py:51
  153.5 41.3 %psum.21 = f32[10,1024]{1,0:T(8,128)S(1)} all-reduce(f32[10,1024]{1,0:T(8,128)S(1)} %convolution_bitcast_fusion), channel_id=1, replica_groups=mesh['centre'=8,'row'=4] {'centre','row'}, use_global_device_ids=true, to_apply=%region_2.3 | all-reduce | flops 10240 | bytes 81920 | tf_op jit(solution)/shard_map/psum | solution.py:55
  194.8 4.0 %gather_fusion.1 = f32[16,1024]{1,0:T(8,128)S(1)} fusion(f32[2048,1024]{1,0:T(8,128)} %copy.17, s32[1024]{0:T(1024)S(1)} %pad_clamp_fusion), kind=kCustom, calls=%fused_computation.1 | custom fusion | bytes 131136 | tf_op jit(solution)/shard_map/jit(_take)/gather | solution.py:52
  198.8 0.8 slice_subtract_fusion
  199.6 0.2 convolution_multiply_fusion.1
  199.9 0.0 copy-done.2
  199.9 0.1 fusion.34
  200.0 40.1 %psum.22 = f32[10,128]{1,0:T(8,128)S(1)} all-reduce(f32[10,128]{1,0:T(8,128)S(1)} %fusion.34), channel_id=1, replica_groups=mesh['centre'=8,'row'=4] {'centre','row'}, use_global_device_ids=true, to_apply=%region_3.4 | all-reduce | flops 1280 | bytes 10240 | tf_op jit(solution)/shard_map/psum | solution.py:71
  240.2 0.1 fusion.6
  240.3 0.1 copy.18
  240.4 31.4 %all_gather.14 = f32[10,512]{0,1:T(8,128)S(1)} all-gather(f32[10,16]{0,1:T(8,128)S(1)} %copy.18), channel_id=1, replica_groups=mesh['centre'=8,'row'=4] {'centre','row'}, dimensions={1}, use_global_device_ids=true | all-gather | bytes 21120 | tf_op jit(solution)/shard_map/all_gather | solution.py:67
  271.7 0.6 fusion.5
  272.3 0.1 fusion.35
  272.4 48.9 %psum.23 = f32[10,128]{1,0:T(8,128)S(1)} all-reduce(f32[10,128]{1,0:T(8,128)S(1)} %fusion.35), channel_id=1, replica_groups=mesh['centre'=8,'row'=4] {'centre','row'}, use_global_device_ids=true, to_apply=%region_5.6 | all-reduce | flops 1280 | bytes 10240 | tf_op jit(solution)/shard_map/psum | solution.py:71
  321.3 0.7 fusion.4
  322.0 0.6 constant_dynamic-slice_fusion
  (7 shorter events, 0.1 us)
Async XLA Ops:
  7.2 136.9 %copy-start = (f32[10,2048]{1,0:T(8,128)S(1)}, f32[10,2048]{1,0:T(8,128)}, u32[]{:S(2)}) copy-start(f32[10,2048]{1,0:T(8,128)} %param.11) | copy-start | bytes 245764
  7.2 59.0 %all-gather.5.cloned.1.call-start = ((), (), s32[]{:S(2)}) async-start(), calls=%async_computation.1 | async-start | bytes 1081344 | tf_op jit(solution)/shard_map/all_gather | solution.py:59
  11.9 55.8 %copy-start.1 = (bf16[16,1024]{1,0:T(8,128)(2,1)S(1)}, bf16[16,1024]{1,0:T(8,128)(2,1)}, u32[]{:S(2)}) copy-start(bf16[16,1024]{1,0:T(8,128)(2,1)} %broadcast_select_fusion) | copy-start | bytes 98308
  12.0 89.5 %all-gather.3.cloned.1.call-start = ((), (), s32[]{:S(2)}) async-start(), calls=%async_computation | async-start | bytes 5324800 | tf_op jit(solution)/shard_map/all_gather | solution.py:45
  144.0 55.9 %copy-start.2 = (f32[16,128]{1,0:T(8,128)S(1)}, f32[16,128]{1,0:T(8,128)}, u32[]{:S(2)}) copy-start(f32[16,128]{1,0:T(8,128)} %param.13) | copy-start | bytes 24580
Sparse Core Ops, SparseCore 0:
  12.1 54.0 all-gather.4
  67.8 33.7 all-gather.2
